TPU v7x, 32 devices: a whole 2x2x4 slice. The times are simulated.
32 devices in a mesh: groups: 2 (over x), dp: 16 (over z, y, core).
Axes of the slice: x: 2, y: 2, z: 4, core: 2. Of those that a mesh axis runs over, the one named last changes fastest.
Arguments:
- latents: bfloat16 [320, 8, 8, 640], P(('groups', 'dp')), parts along dimension 0, may hold values from -6 to 6
- targets: bfloat16 [320, 8, 8, 320], P(('groups', 'dp')), parts along dimension 0, may hold values from -6 to 6
- heights: int32 [320], P('groups'), parts along dimension 0, may hold values from 4 to 8
- widths: int32 [320], P('groups'), parts along dimension 0, may hold values from 4 to 8
- owner: int32 [320], P('groups'), parts along dimension 0, may hold values from -1 to 15, as said below
- weight: bfloat16 [5760, 320], P('dp'), may hold values from -0.078125 to 0.078125
- probe: bfloat16 [11520, 320], P(('groups', 'dp')), parts along dimension 0, may hold values from -0.078125 to 0.078125
Outputs:
- hvp: float32 [11520, 320], P(('groups', 'dp')), parts along dimension 0
There are 2 independent parts, one for each index of `groups`. A program takes and returns all parts, laid end to end along the dimension named above; an argument that names none is the same for every part. Nothing has to cross between parts.
Inputs may be any that keep to these rules, and one draw needn't show every extreme that they name: Slot s lies on device s // 10 of dp. owner[s] is -1 for an empty slot, else that device or its partner, the device whose index differs in the lowest bit. Every device owns exactly 5 samples. In every draw some device holds 10 filled slots, 5 of them owned by its partner.
All inputs are finite; a program needn't handle non-finite values.
Results may differ from a plain program's by a relative error of at most 0.0039.
Values may be sent and summed in bfloat16 or wider, within the bound.
A program may use at most 64 MiB of HBM per device.

v0:
```python
import jax
import jax.numpy as jnp
from jax import lax
from jax.sharding import PartitionSpec as P

CHANNELS = 640
GROUPS = 32


EPSILON = 1e-05


def partner_2(value, axis, stride):
    mask = 2**stride
    pairs = [(source, source ^ mask) for source in range(lax.axis_size(axis))]
    return lax.ppermute(value, axis, pairs)


def group_onehot(channels):
    per_group = CHANNELS // GROUPS
    group_count = channels // per_group
    return (jnp.arange(channels)[:, None] // per_group == jnp.arange(group_count)[None, :]).astype(
        jnp.float32
    )


def group_norm(values, spatial):
    channels = values.shape[-1]
    onehot = group_onehot(channels)
    highest = lax.Precision.HIGHEST
    pixel_weights = spatial[:, :, :, None]
    counts = jnp.sum(spatial, axis=(1, 2)) * (CHANNELS // GROUPS)
    group_sums = jnp.dot(jnp.sum(values * pixel_weights, axis=(1, 2)), onehot, precision=highest)
    channel_mean = jnp.dot(group_sums / counts[:, None], onehot.T, precision=highest)
    centred = values - channel_mean[:, None, None, :]
    group_squares = jnp.dot(
        jnp.sum(centred * centred * pixel_weights, axis=(1, 2)), onehot, precision=highest
    )
    channel_scale = jnp.dot(
        lax.rsqrt(group_squares / counts[:, None] + EPSILON), onehot.T, precision=highest
    )
    return centred * channel_scale[:, None, None, :]


def frame_mask(heights, widths, frame_rows, frame_cols):
    inside_rows = jnp.arange(frame_rows, dtype=jnp.int32)[None, :] < heights[:, None]
    inside_cols = jnp.arange(frame_cols, dtype=jnp.int32)[None, :] < widths[:, None]
    return (inside_rows[:, :, None] & inside_cols[:, None, :]).astype(jnp.float32)


def unfold(hidden):
    samples, frame_rows, frame_cols, channels = hidden.shape
    padded = jnp.pad(hidden, ((0, 0), (1, 1), (1, 1), (0, 0)))
    shifted = [
        padded[:, offset_row : offset_row + frame_rows, offset_col : offset_col + frame_cols, :]
        for offset_row in range(3)
        for offset_col in range(3)
    ]
    return jnp.concatenate(shifted, axis=-1).reshape(
        samples * frame_rows * frame_cols, 9 * channels
    )


def second_order(pre_norm, tangent, wanted, spatial, live_flag, factor):
    loss_weights = (spatial * live_flag[:, None, None])[:, :, :, None]

    def loss_value(values):
        activated = jax.nn.silu(group_norm(values, spatial))
        missing = activated - wanted
        return 0.5 * factor * jnp.sum(loss_weights * missing * missing)

    def along_tangent(values):
        return jnp.sum(jax.grad(loss_value)(values) * tangent)

    return jax.grad(along_tangent)(pre_norm)


def first_slots(flags, owned):
    slot_count = flags.shape[0]
    position = jnp.arange(slot_count, dtype=jnp.int32)
    ordering = jnp.argsort(jnp.where(flags, position, position + slot_count))
    return ordering[:owned]


def per_device(latents, targets, heights, widths, owner, weight, probe):
    slot_count = latents.shape[0]
    owned = slot_count // 2
    my_index = lax.axis_index("dp")
    factor = 1.0 / (owned * lax.axis_size("dp"))
    my_owner = lax.dynamic_slice_in_dim(owner, my_index * slot_count, slot_count)
    my_heights = lax.dynamic_slice_in_dim(heights, my_index * slot_count, slot_count)
    my_widths = lax.dynamic_slice_in_dim(widths, my_index * slot_count, slot_count)
    partner = jnp.bitwise_xor(my_index, 1)
    keep_pick = first_slots(my_owner == my_index, owned)
    send_pick = first_slots(my_owner == partner, owned)
    outgoing = (jnp.take(latents, send_pick, axis=0), jnp.take(targets, send_pick, axis=0))
    incoming = partner_2((outgoing[0], outgoing[1]), "dp", 0)
    their_owner = lax.dynamic_slice_in_dim(owner, partner * slot_count, slot_count)
    their_heights = lax.dynamic_slice_in_dim(heights, partner * slot_count, slot_count)
    their_widths = lax.dynamic_slice_in_dim(widths, partner * slot_count, slot_count)
    recv_pick = first_slots(their_owner == my_index, owned)[::-1]
    kept_count = jnp.sum((my_owner == my_index).astype(jnp.int32))
    from_self = jnp.arange(owned, dtype=jnp.int32) < kept_count
    frame_pick = from_self[:, None, None, None]
    frames = jnp.where(frame_pick, jnp.take(latents, keep_pick, axis=0), incoming[0][::-1])
    wanted = jnp.where(frame_pick, jnp.take(targets, keep_pick, axis=0), incoming[1][::-1])
    sample_heights = jnp.where(
        from_self, jnp.take(my_heights, keep_pick), jnp.take(their_heights, recv_pick)
    )
    sample_widths = jnp.where(
        from_self, jnp.take(my_widths, keep_pick), jnp.take(their_widths, recv_pick)
    )
    live_flag = jnp.where(
        from_self,
        jnp.take(my_owner, keep_pick) == my_index,
        jnp.take(their_owner, recv_pick) == my_index,
    ).astype(jnp.float32)
    spatial = frame_mask(sample_heights, sample_widths, frames.shape[1], frames.shape[2])
    hidden = (
        jax.nn.silu(group_norm(frames.astype(jnp.float32), spatial)) * spatial[:, :, :, None]
    ).astype(jnp.bfloat16)
    patches = unfold(hidden)
    out_channels = weight.shape[1]

    def add_rows(shard_rows):
        return jnp.dot(patches, shard_rows, preferred_element_type=jnp.float32)

    forward = add_rows(lax.all_gather(weight, "dp", axis=0, tiled=True))
    tangent = add_rows(lax.all_gather(probe, "dp", axis=0, tiled=True))
    field_shape = frames.shape[:3] + (out_channels,)
    forward = forward.reshape(field_shape)
    tangent = tangent.reshape(field_shape)
    wanted_float = wanted.astype(jnp.float32)
    part_curv = second_order(forward, tangent, wanted_float, spatial, live_flag, factor)
    curvature = part_curv.astype(jnp.bfloat16).reshape(-1, out_channels - 0)
    return lax.psum_scatter(
        lax.dot_general(
            patches, curvature, (((0,), (0,)), ((), ())), preferred_element_type=jnp.float32
        ),
        "dp",
        scatter_dimension=0,
        tiled=True,
    )


def solution(mesh):
    return jax.shard_map(
        per_device,
        mesh=mesh,
        in_specs=(
            P(("groups", "dp"), None, None, None),
            P(("groups", "dp"), None, None, None),
            P("groups"),
            P("groups"),
            P("groups"),
            P("dp", None),
            P(("groups", "dp"), None),
        ),
        out_specs=P(("groups", "dp"), None),
        check_vma=False,
    )
```

profile of v0, /device:TPU:31, one launch (start us, length us, event | category | flops | bytes accessed | tf_op | source)
XLA Modules:
  0.0 308.2 jit_solution(2530066521305687888)
XLA Ops:
  8.1 1.5 fusion.88
  9.6 1.3 sort.46
  12.3 1.6 gather_fusion.9
  14.2 1.3 sort.45
  18.7 1.3 sort.47
  26.7 0.9 fusion.36
  28.4 0.9 fusion.38
  29.3 0.9 fusion.39
  30.2 1.1 constant_dynamic-update-slice_fusion
  31.2 0.9 fusion.40
  32.1 0.9 fusion.41
  33.9 0.9 fusion.43
  34.7 23.5 %all-gather.7.cloned.1.call-done = bf16[16,360,320]{1,2,0:T(8,128)(2,1)} async-done(((bf16[1,360,320]{1,2,0:T(8,128)(2,1)}), bf16[16,360,320]{1,2,0:T(8,128)(2,1)}) %all-gather.7.cloned.1.call-update) | async-done | bytes 3686416 | tf_op jit(solution)/shard_map/all_gather | solution.py:129
  58.3 6.4 %copy.13 = bf16[16,360,320]{1,0,2:T(8,128)(2,1)} copy(bf16[16,360,320]{1,2,0:T(8,128)(2,1)} %all-gather.7.cloned.1.call-done) | data formatting | bytes 7372800 | tf_op jit(solution)/shard_map/all_gather | solution.py:129
  64.7 7.8 %reshape.249 = bf16[5760,320,1,1]{0,1,2,3:T(8,128)(2,1)} reshape(bf16[16,360,320]{1,0,2:T(8,128)(2,1)} %copy.13) | data formatting | bytes 7372800
  72.4 36.0 %all-gather.5.cloned.1.call-done = bf16[16,360,320]{1,2,0:T(8,128)(2,1)} async-done(((bf16[1,360,320]{1,2,0:T(8,128)(2,1)}), bf16[16,360,320]{1,2,0:T(8,128)(2,1)}) %all-gather.5.cloned.1.call-update) | async-done | bytes 3686416 | tf_op jit(solution)/shard_map/all_gather | solution.py:128
  108.5 6.4 %copy.12 = bf16[16,360,320]{1,0,2:T(8,128)(2,1)} copy(bf16[16,360,320]{1,2,0:T(8,128)(2,1)} %all-gather.5.cloned.1.call-done) | data formatting | bytes 7372800 | tf_op jit(solution)/shard_map/all_gather | solution.py:128
  114.8 7.7 %reshape.248 = bf16[5760,320,1,1]{0,1,2,3:T(8,128)(2,1)} reshape(bf16[16,360,320]{1,0,2:T(8,128)(2,1)} %copy.12) | data formatting | bytes 7372800
  122.6 5.4 %fusion = f32[5,8,8,320]{3,2,1,0:T(8,128)S(1)} fusion(bf16[5,8,8,5760]{3,2,1,0:T(8,128)(2,1)} %fusion.43, bf16[5760,320,1,1]{0,1,2,3:T(8,128)(2,1)} %reshape.249), kind=kOutput, calls=%fused_computation.11 | convolution fusion | flops 1179648000 | bytes 7782400 | tf_op jit(solution)/shard_map/dot_general | solution.py:126
  128.0 4.2 %multiply_reduce_fusion.5 = (f32[5,320]{1,0:T(8,128)S(1)}, f32[5,320]{1,0:T(8,128)S(1)}, f32[5,8,8,320]{3,2,1,0:T(8,128)S(1)}) fusion(f32[5,8,8]{2,1,0:T(8,128)S(1)} %and_convert_fusion, f32[5,8,8,320]{3,2,1,0:T(8,128)S(1)} %fusion, bf16[5,8,8,5760]{3,2,1,0:T(8,128)(2,1)} %fusion.43, bf16[5760,320,1,1]{0,1,2,3:T(8,128)(2,1)S(1)} %copy-done.1), kind=kOutput, calls=%fused_computation.80 | convolution fusion | flops 1180054528 | bytes 8206080 | tf_op jit(solution)/shard_map/dot_general | solution.py:126
  134.5 1.2 multiply_reduce_fusion
  137.7 7.3 %convolution_bitcast_fusion = f32[5760,320]{0,1:T(8,128)} fusion(bf16[5,8,8,5760]{3,2,1,0:T(8,128)(2,1)} %fusion.43, f32[5,8,8,320]{3,2,1,0:T(8,128)S(1)} %get-tuple-element.22, f32[5,320]{1,0:T(8,128)S(1)} %fusion.48, f32[5,8,8]{2,1,0:T(8,128)S(1)} %and_convert_fusion), kind=kOutput, calls=%fused_computation.10 | convolution fusion | flops 1179955200 | bytes 11476480 | tf_op jit(solution)/shard_map/dot_general | solution.py:137
  146.8 152.8 %all-reduce.4.cloned.1.call-done = f32[5760,320]{0,1:T(8,128)} async-done(((f32[5760,320]{0,1:T(8,128)}), f32[5760,320]{0,1:T(8,128)}) %all-reduce.4.cloned.1.call-update) | async-done | bytes 7372816
  299.7 2.0 constant_dynamic-slice_fusion
  (79 shorter events, 20.3 us)
Async XLA Ops:
  6.5 4.3 %copy-start = (bf16[10,8,8,640]{3,2,1,0:T(8,128)(2,1)S(1)}, bf16[10,8,8,640]{3,2,1,0:T(8,128)(2,1)}, u32[]{:S(2)}) copy-start(bf16[10,8,8,640]{3,2,1,0:T(8,128)(2,1)} %param.13) | copy-start | bytes 2457604
  6.5 10.2 %copy-start.2 = (bf16[10,8,8,320]{3,2,1,0:T(8,128)(2,1)S(1)}, bf16[10,8,8,320]{3,2,1,0:T(8,128)(2,1)}, u32[]{:S(2)}) copy-start(bf16[10,8,8,320]{3,2,1,0:T(8,128)(2,1)} %param.14) | copy-start | bytes 1228804
  6.5 11.5 %copy-start.3 = (s32[160]{0:T(256)S(1)}, s32[160]{0:T(256)}, u32[]{:S(2)}) copy-start(s32[160]{0:T(256)} %param.16) | copy-start | bytes 1924
  6.5 51.7 %all-gather.7.cloned.1.call-start = ((), (), s32[]{:S(2)}) async-start(), calls=%async_computation.1 | async-start | bytes 4177920 | tf_op jit(solution)/shard_map/all_gather | solution.py:129
  7.3 101.2 %all-gather.5.cloned.1.call-start = ((), (), s32[]{:S(2)}) async-start(), calls=%async_computation | async-start | bytes 4177920 | tf_op jit(solution)/shard_map/all_gather | solution.py:128
  8.0 291.7 %all-reduce.4.cloned.1.call-start = ((), (), s32[]{:S(2)}) async-start(), calls=%async_computation.2 | async-start | bytes 14745600
  11.6 12.9 %collective-permute-start = (bf16[5,8,8,640]{3,2,1,0:T(8,128)(2,1)S(1)}, bf16[5,8,8,640]{3,2,1,0:T(8,128)(2,1)S(1)}, u32[]{:S(2)}, u32[]{:S(2)}) collective-permute-start(bf16[5,8,8,640]{3,2,1,0:T(8,128)(2,1)S(1)} %broadcast_select_fusion), channel_id=1, source_target_pairs={{0,1},{1,0},{2,3},{3,2},{4,5},{5,4},{6,7},{7,6},{8,9},{9,8},{10,11... | collective-permute-start | bytes 1228808 | tf_op jit(solution)/shard_map/ppermute | solution.py:16
  14.1 120.4 %collective-permute-start.1 = (bf16[5,8,8,320]{3,2,1,0:T(8,128)(2,1)S(1)}, bf16[5,8,8,320]{3,2,1,0:T(8,128)(2,1)S(1)}, u32[]{:S(2)}, u32[]{:S(2)}) collective-permute-start(bf16[5,8,8,320]{3,2,1,0:T(8,128)(2,1)S(1)} %broadcast_select_fusion.1), channel_id=1, source_target_pairs={{0,1},{1,0},{2,3},{3,2},{4,5},{5,4},{6,7},{7,6},{8,9},{9,8},{10,11... | collective-permute-start | bytes 614408 | tf_op jit(solution)/shard_map/ppermute | solution.py:16
  122.6 5.4 %copy-start.1 = (bf16[5760,320,1,1]{0,1,2,3:T(8,128)(2,1)S(1)}, bf16[5760,320,1,1]{0,1,2,3:T(8,128)(2,1)}, u32[]{:S(2)}) copy-start(bf16[5760,320,1,1]{0,1,2,3:T(8,128)(2,1)} %reshape.248) | copy-start | bytes 11059204
  145.0 0.7 copy-start.4
Sparse Core Ops, SparseCore 0:
  9.6 48.5 all-gather.6
  60.5 47.8 all-gather.4
  145.1 154.5 all-reduce.3
where the time goes:
time: 312 us; the launch traced here: 308 us
  waiting for transfers between devices  214 us (69%)
  local copies, waits for them, and re-layouts  46 us (15%)
  matrix products  21.9 us (7%)
  between operations  14 us (4%)
  other arithmetic  11.6 us (4%)
    unnamed x4, waiting for transfers between devices  154 us
    all_gather x1, waiting for transfers between devices, per_device(): forward = add_rows(lax.all_gather(weight, 'dp', axis=0, tiled=True))  36 us
    unnamed x21, local copies, waits for them, and re-layouts  24.8 us
    all_gather x1, waiting for transfers between devices, per_device(): tangent = add_rows(lax.all_gather(probe, 'dp', axis=0, tiled=True))  23.5 us
    dot_general x2, matrix products, add_rows(): return jnp.dot(patches, shard_rows, preferred_element_type=jnp.float32)  9.54 us
    dot_general x1, matrix products, per_device(): lax.dot_general(patches, curvature, (((0,), (0,)), ((), ())), preferred_e...  7.3 us
    all_gather x1, local copies, waits for them, and re-layouts, per_device(): tangent = add_rows(lax.all_gather(probe, 'dp', axis=0, tiled=True))  6.41 us
    all_gather x1, local copies, waits for them, and re-layouts, per_device(): forward = add_rows(lax.all_gather(weight, 'dp', axis=0, tiled=True))  6.38 us
  transfers between devices with their start and end apart: 5, of which 3 were waited for; matrix products, arithmetic and copies ran while one was open for 22% of the time, Pallas kernels for 0%

commit v1 on v0

v1 whole, which is shorter than its diff:
```python
import functools

import jax
import jax.numpy as jnp
from jax import lax
from jax.experimental import pallas as pl
from jax.experimental.pallas import tpu as pltpu
from jax.sharding import PartitionSpec as P

PER_GROUP = 20
EPSILON = 1e-05
BLOCK = 8
CHIPS = BLOCK // 2
CELLS = 64
LANES = 128
MESH = pl.DeviceIdType.MESH
F32 = jnp.float32
BF16 = jnp.bfloat16


def up(value, step):
    return -(-value // step) * step


def thirds(value):
    high = value.astype(BF16)
    rest = value - high.astype(F32)
    mid = rest.astype(BF16)
    low = (rest - mid.astype(F32)).astype(BF16)
    return high, mid, low


def times_onehot(value, onehot):
    rows = value.shape[0]
    stacked = jnp.concatenate(
        [part.astype(F32) for part in thirds(value)], axis=0
    ).astype(BF16)
    product = jnp.dot(stacked, onehot, preferred_element_type=F32)
    return product[:rows] + product[rows : 2 * rows] + product[2 * rows :]


def onehot_times(onehot, value):
    high, mid, low = thirds(value)
    dot = functools.partial(jnp.dot, preferred_element_type=F32)
    return dot(onehot, high) + dot(onehot, mid) + dot(onehot, low)


def between(inner, outer, width):
    return (inner >= outer * width) & (inner < outer * width + width)


def iota(shape, axis):
    return lax.broadcasted_iota(jnp.int32, shape, axis)


def window_of(start, width, total):
    size = min(up(width + LANES - 1, LANES), total)
    return min(start // LANES * LANES, total - size), size


def kernel(
    n, factor, pick, high, wide, lat_in, tgt_in, w_in, mask_in, out,
    lat, tgt, w_buf, w_flat, wall, hid, t_out, t_buf, z, u_buf, t_tan, curv, acc, r_out, r_buf,
    lat_send, lat_recv, tgt_send, tgt_recv, w_send, w_recv, h_send, h_recv, t_send, t_recv,
    r_send, r_recv,
):
    me = lax.axis_index("dp")
    pos = lax.rem(me, BLOCK)
    base = me - pos
    chip = pos // 2
    core = lax.rem(pos, 2)
    partner = me + 1 - 2 * core
    slots = lat_in.shape[0]
    owned = slots // 2
    pair = 2 * owned
    width = pair * CELLS
    half = owned * CELLS
    channels = lat_in.shape[2]
    rows = w_rows = out.shape[1]
    del w_rows
    cols = out.shape[0] // BLOCK
    kernel_rows = w_flat.shape[1]
    share = kernel_rows // n

    barrier = pltpu.get_barrier_semaphore()

    def greet(k, _):
        pl.semaphore_signal(
            barrier, inc=1, device_id={"dp": lax.rem(me + k, n)}, device_id_type=MESH
        )
        return 0

    lax.fori_loop(1, n, greet, 0)
    pl.semaphore_wait(barrier, n - 1)

    def remote(src, dst, send, recv, target):
        return pltpu.make_async_remote_copy(
            src_ref=src, dst_ref=dst, send_sem=send, recv_sem=recv,
            device_id={"dp": target}, device_id_type=MESH,
        )

    lat_copy = remote(lat_in, lat.at[core], lat_send, lat_recv, partner)
    lat_copy.start()
    tgt_copy = remote(tgt_in, tgt.at[core], tgt_send, tgt_recv, partner)
    tgt_copy.start()

    def send_w(k, _):
        target = lax.rem(me + k, n)
        remote(w_in.at[lax.rem(target, BLOCK)], w_buf.at[me], w_send, w_recv, target).start()
        return 0

    lax.fori_loop(1, n, send_w, 0)
    w_own = pltpu.make_async_copy(w_in.at[pos], w_buf.at[me], w_recv)
    w_own.start()
    lat[core] = lat_in[...]
    tgt[core] = tgt_in[...]
    lat_copy.wait_recv()

    to_group = between(
        iota((channels, LANES), 0), iota((channels, LANES), 1), PER_GROUP
    ).astype(F32).astype(BF16)
    from_group = between(
        iota((LANES, channels), 1), iota((LANES, channels), 0), PER_GROUP
    ).astype(F32).astype(BF16)
    cell = iota((CELLS, channels), 0)
    cell_row, cell_col = cell >> 3, cell & 7
    frames, inside, counts = [], [], []
    for k in range(owned):
        which = pick[core * owned + k]
        tall, broad = high[core * owned + k], wide[core * owned + k]
        frames.append(lat[which // slots, lax.rem(which, slots)].astype(F32))
        inside.append(((cell_row < tall) & (cell_col < broad)).astype(F32))
        counts.append(jnp.full((1, LANES), tall * broad * PER_GROUP, jnp.int32).astype(F32))
    spare = 8 - owned
    counts = jnp.concatenate(counts + [jnp.ones((spare, LANES), F32)], axis=0)

    def group_mean(values):
        sums = [jnp.sum(v * m, axis=0, keepdims=True) for v, m in zip(values, inside)]
        sums = jnp.concatenate(sums + [jnp.zeros((spare, channels), F32)], axis=0)
        return times_onehot(sums, to_group) / counts

    mean = times_onehot(group_mean(frames), from_group)
    centred = [v - mean[k : k + 1] for k, v in enumerate(frames)]
    square = group_mean([v * v for v in centred])
    scale = times_onehot(lax.rsqrt(square + EPSILON), from_group)
    for k in range(owned):
        x = centred[k] * scale[k : k + 1]
        hid[pos, k * CELLS : (k + 1) * CELLS] = (
            x / (1.0 + jnp.exp(-x)) * inside[k]
        ).astype(BF16)

    def send_hidden(k, _):
        target = base + lax.rem(pos + k, BLOCK)
        remote(hid.at[pos], hid.at[pos], h_send, h_recv, target).start()
        return 0

    lax.fori_loop(1, BLOCK, send_hidden, 0)

    tgt_copy.wait_recv()
    chosen = []
    for k in range(pair):
        which = pick[k]
        chosen.append(tgt[which // slots, lax.rem(which, slots)].astype(F32))
    turned = jnp.concatenate(chosen, axis=0).T
    t_rows = t_out.shape[1]
    for b in range(BLOCK):
        t_out[b] = jnp.concatenate(
            [turned[b * cols : (b + 1) * cols], jnp.zeros((t_rows - cols, width), F32)], axis=0
        ).astype(BF16)
    t_buf[chip] = t_out[pos]

    def send_targets(k, _):
        there = 2 * lax.rem(chip + k, CHIPS) + core
        remote(t_out.at[there], t_buf.at[chip], t_send, t_recv, base + there).start()
        return 0

    lax.fori_loop(1, CHIPS, send_targets, 0)

    remote(w_buf, w_buf, w_send, w_recv, partner).wait_recv()
    w_flat[...] = jnp.zeros_like(w_flat)
    for d in range(n):
        start, size = window_of(d * share, share, kernel_rows)
        piece = w_buf[d].astype(F32)
        lane = iota(piece.shape, 1)
        piece = jnp.where(lane < share, piece, 0.0)
        if size > rows:
            piece = jnp.concatenate(
                [piece, jnp.zeros((piece.shape[0], size - rows), F32)], axis=1
            )
        if d * share > start:
            piece = pltpu.roll(piece, d * share - start, 1)
        w_flat[:, start : start + size] += piece
    both = 2 * cols
    for tap in range(9):
        wall[tap * both : (tap + 1) * both] = w_flat[
            :, tap * channels : (tap + 1) * channels
        ].astype(BF16)

    lane = iota((1, width), 1)
    lane_row, lane_col = (lane >> 3) & 7, lane & 7

    def tap_of(tap):
        a, b = tap // 3 - 1, tap % 3 - 1
        valid = (
            (lane_row + a >= 0) & (lane_row + a < 8) & (lane_col + b >= 0) & (lane_col + b < 8)
        )
        return a * 8 + b, valid.astype(F32)

    remote(
        hid.at[pl.ds(0, BLOCK - 1)], hid.at[pl.ds(0, BLOCK - 1)], h_send, h_recv, partner
    ).wait_recv()

    def forward(q, _):
        features = hid[pl.ds(2 * q, 2)].reshape(width, channels)
        z[...] = lax.dot_general(
            wall[...], features, (((1,), (1,)), ((), ())), preferred_element_type=F32
        )
        total = z[4 * both : 5 * both]
        for tap in range(9):
            if tap != 4:
                offset, valid = tap_of(tap)
                total = total + valid * pltpu.roll(
                    z[tap * both : (tap + 1) * both], -offset % width, 1
                )
        u_buf[q] = total[:cols]
        t_tan[q] = total[cols:]
        return 0

    lax.fori_loop(0, CHIPS, forward, 0)
    remote(
        t_buf.at[pl.ds(0, CHIPS - 1)], t_buf.at[pl.ds(0, CHIPS - 1)], t_send, t_recv, partner
    ).wait_recv()

    wide_rows = CHIPS * cols
    to_sample = between(
        iota((width, LANES), 0), iota((width, LANES), 1), CELLS
    ).astype(F32).astype(BF16)
    from_sample = between(
        iota((LANES, width), 1), iota((LANES, width), 0), CELLS
    ).astype(F32).astype(BF16)
    row, col = iota((wide_rows, LANES), 0), iota((wide_rows, LANES), 1)
    to_norm = between(row, col, PER_GROUP).astype(F32).astype(BF16)
    row, col = iota((LANES, wide_rows), 1), iota((LANES, wide_rows), 0)
    of_norm = between(row, col, PER_GROUP).astype(F32).astype(BF16)
    mask = jnp.concatenate(
        [jnp.broadcast_to(mask_in[q, 0:1], (cols, width)) for q in range(CHIPS)], axis=0
    )
    per_sample = jnp.dot(mask.astype(BF16), to_sample, preferred_element_type=F32)
    inverse = 1.0 / (jnp.maximum(per_sample, 1.0) * PER_GROUP)

    def small(value):
        return onehot_times(to_norm, onehot_times(of_norm, times_onehot(value, to_sample))) * inverse

    def spread(value):
        return times_onehot(value, from_sample)

    u = u_buf[...].reshape(wide_rows, width)
    t = t_tan[...].reshape(wide_rows, width)
    c = u - spread(small(u * mask))
    r = spread(lax.rsqrt(small(c * c * mask) + EPSILON))
    x = c * r
    wanted = jnp.concatenate([t_buf[q].astype(F32)[:cols] for q in range(CHIPS)], axis=0)
    a = spread(small(x * t * mask))
    x_dot = r * (t - spread(small(t * mask)) - x * a)
    sigma = 1.0 / (1.0 + jnp.exp(-x))
    missing = x * sigma - wanted
    first = sigma * (1.0 + x * (1.0 - sigma))
    second = sigma * (1.0 - sigma) * (2.0 + x * (1.0 - 2.0 * sigma))
    weight = factor * mask
    g = weight * missing * first
    g_dot = weight * (first * first + missing * second) * x_dot
    b = spread(small(g * x))
    h = g - spread(small(g)) - x * b
    h_dot = g_dot - spread(small(g_dot)) - x_dot * b - x * spread(small(g_dot * x + g * x_dot))
    result = mask * (r * h_dot - r * r * a * h)
    curv[...] = result.reshape(CHIPS, cols, width)

    acc[...] = jnp.zeros_like(acc)

    def backward(q, _):
        values = curv[q]
        shifted = []
        for tap in range(9):
            offset, valid = tap_of(tap)
            term = values * valid
            shifted.append(term if offset == 0 else pltpu.roll(term, offset % width, 1))
        features = hid[pl.ds(2 * q, 2)].reshape(width, channels)
        acc[...] += jnp.dot(
            jnp.concatenate(shifted, axis=0).astype(BF16), features, preferred_element_type=F32
        )
        return 0

    lax.fori_loop(0, CHIPS, backward, 0)
    flat = w_flat
    for tap in range(9):
        flat[:cols, tap * channels : (tap + 1) * channels] = acc[tap * cols : (tap + 1) * cols]
    r_rows = r_out.shape[1]
    for d in range(n):
        start, size = window_of(d * share, share, kernel_rows)
        piece = flat[: r_rows, start : start + size]
        if d * share > start:
            piece = pltpu.roll(piece, (start - d * share) % size, 1)
        r_out[d] = piece[:, :rows].astype(BF16)

    def send_sums(k, _):
        target = lax.rem(me + k, n)
        remote(r_out.at[target], r_buf.at[me], r_send, r_recv, target).start()
        return 0

    lax.fori_loop(1, n, send_sums, 0)
    r_own = pltpu.make_async_copy(r_out.at[me], r_buf.at[me], r_recv)
    r_own.start()
    remote(r_buf, r_buf, r_send, r_recv, partner).wait_recv()
    for b in range(BLOCK):
        total = r_buf[b].astype(F32)
        for other in range(b + BLOCK, n, BLOCK):
            total = total + r_buf[other].astype(F32)
        out[b * cols : (b + 1) * cols] = total[:cols]

    lat_copy.wait_send()
    tgt_copy.wait_send()
    others = pl.ds(0, n - 1)
    remote(w_buf.at[others], w_buf.at[others], w_send, w_recv, partner).wait_send()
    peers = pl.ds(0, BLOCK - 1)
    remote(hid.at[peers], hid.at[peers], h_send, h_recv, partner).wait_send()
    chips = pl.ds(0, CHIPS - 1)
    remote(t_buf.at[chips], t_buf.at[chips], t_send, t_recv, partner).wait_send()
    remote(r_buf.at[others], r_buf.at[others], r_send, r_recv, partner).wait_send()


def per_device(latents, targets, heights, widths, owner, weight, probe):
    n = lax.axis_size("dp")
    slots, frame_rows, frame_cols, channels = latents.shape
    cells = frame_rows * frame_cols
    share, out_channels = weight.shape
    owned = slots // 2
    pair = 2 * owned
    width = pair * cells
    cols = out_channels // BLOCK
    rows = up(share, LANES)
    kernel_rows = share * n
    me = lax.axis_index("dp")
    base = me // BLOCK * BLOCK

    def of_block(values):
        return lax.dynamic_slice_in_dim(values, base * slots, BLOCK * slots).reshape(
            CHIPS, 2 * slots
        )

    live = of_block(owner) >= 0
    index = jnp.arange(2 * slots, dtype=jnp.int32)
    before = index[None, :] < index[:, None]
    rank = jnp.sum((live[:, None, :] & before[None]).astype(jnp.int32), axis=2)
    taken = (
        (rank[:, None, :] == jnp.arange(pair, dtype=jnp.int32)[None, :, None]) & live[:, None, :]
    ).astype(jnp.int32)
    slot = jnp.sum(taken * index[None, None, :], axis=2)
    tall = jnp.sum(taken * of_block(heights)[:, None, :], axis=2)
    broad = jnp.sum(taken * of_block(widths)[:, None, :], axis=2)
    place = jnp.arange(cells, dtype=jnp.int32)
    mask = (
        (place[None, None, :] // frame_cols < tall[:, :, None])
        & (place[None, None, :] % frame_cols < broad[:, :, None])
    ).astype(F32)
    mask = jnp.broadcast_to(mask.reshape(CHIPS, 1, width), (CHIPS, 8, width))
    chip = (me - base) // 2

    def mine(values):
        return lax.dynamic_index_in_dim(values, chip, 0, keepdims=False)

    both = jnp.concatenate(
        [weight.T.reshape(BLOCK, cols, share), probe.T.reshape(BLOCK, cols, share)], axis=1
    )
    both = jnp.pad(both, ((0, 0), (0, 0), (0, rows - share)))
    padded = up(cols, 16)
    smem = pl.BlockSpec(memory_space=pltpu.SMEM)
    vmem = pl.BlockSpec(memory_space=pltpu.VMEM)
    sem = pltpu.SemaphoreType.DMA
    scratch = [
        pltpu.VMEM((2, slots, cells, channels), BF16),
        pltpu.VMEM((2, slots, cells, out_channels), BF16),
        pltpu.VMEM((n, 2 * cols, rows), BF16),
        pltpu.VMEM((2 * cols, kernel_rows), F32),
        pltpu.VMEM((9 * 2 * cols, channels), BF16),
        pltpu.VMEM((BLOCK, owned * cells, channels), BF16),
        pltpu.VMEM((BLOCK, padded, width), BF16),
        pltpu.VMEM((CHIPS, padded, width), BF16),
        pltpu.VMEM((9 * 2 * cols, width), F32),
        pltpu.VMEM((CHIPS, cols, width), F32),
        pltpu.VMEM((CHIPS, cols, width), F32),
        pltpu.VMEM((CHIPS, cols, width), F32),
        pltpu.VMEM((9 * cols, channels), F32),
        pltpu.VMEM((n, padded, rows), BF16),
        pltpu.VMEM((n, padded, rows), BF16),
    ] + [sem] * 12
    turned = pl.pallas_call(
        functools.partial(kernel, n, 1.0 / (owned * n)),
        out_shape=jax.ShapeDtypeStruct((out_channels, rows), F32),
        in_specs=[smem] * 3 + [vmem] * 4,
        out_specs=vmem,
        scratch_shapes=scratch,
        compiler_params=pltpu.CompilerParams(
            collective_id=0, has_side_effects=True, vmem_limit_bytes=56 * 2**20
        ),
    )(
        mine(slot),
        mine(tall),
        mine(broad),
        latents.reshape(slots, cells, channels),
        targets.reshape(slots, cells, out_channels),
        both,
        mask,
    )
    return turned[:, :share].T


def solution(mesh):
    return jax.shard_map(
        per_device,
        mesh=mesh,
        in_specs=(
            P(("groups", "dp"), None, None, None),
            P(("groups", "dp"), None, None, None),
            P("groups"),
            P("groups"),
            P("groups"),
            P("dp", None),
            P(("groups", "dp"), None),
        ),
        out_specs=P(("groups", "dp"), None),
        check_vma=False,
    )
```

time: 312 us -> 96.4 us (0.31); the launches traced: 308 us -> 96 us
  waiting for transfers between devices: 214 us -> 0 us
  Pallas kernels: 0 us -> 88.2 us
  local copies, waits for them, and re-layouts: 46 us -> 5.75 us
  matrix products: 21.9 us -> 0 us
  between operations: 14 us -> 0.07 us
  other arithmetic: 11.6 us -> 1.96 us
    unnamed x4 -> x0, waiting for transfers between devices: 154 us -> none
    pallas_call x0 -> x1, Pallas kernels: none -> 88.2 us  [per_device(): pl.pallas_call(functools.partial(kernel, n, 1.0 / (owned * n)), out_shape...]
    all_gather x2 -> x0, waiting for transfers between devices: 59.5 us -> none  [the longest x1 36 us: per_device(): forward = add_rows(lax.all_gather(weight, 'dp', axis=0, tiled=True))]
    unnamed x21 -> x10, local copies, waits for them, and re-layouts: 24.8 us -> 0.65 us
    dot_general x21 -> x0, matrix products: 21.9 us -> none  [the longest x2 9.54 us: add_rows(): return jnp.dot(patches, shard_rows, preferred_element_type=jnp.float32)]
    all_gather x2 -> x0, local copies, waits for them, and re-layouts: 12.8 us -> none  [the longest x1 6.41 us: per_device(): tangent = add_rows(lax.all_gather(probe, 'dp', axis=0, tiled=True))]
    gather x10 -> x0, local copies, waits for them, and re-layouts: 7.35 us -> none  [the longest x1 1.63 us: per_device(): jnp.take(targets, send_pick, axis=0)]
    sort x3 -> x0, other arithmetic: 3.83 us -> none  [first_slots(): ordering = jnp.argsort(jnp.where(flags, position, position + slot_count))]
  transfers between devices with their start and end apart: 5 -> 0, of which waited for: 3 -> 0; matrix products, arithmetic and copies ran while one was open for 22% -> 0% of each run, Pallas kernels for 0% -> 0%
where the time goes in v1:
time: 96.4 us; the launch traced here: 96 us
  Pallas kernels  88.2 us (91%)
  local copies, waits for them, and re-layouts  5.75 us (6%)
  other arithmetic  1.96 us (2%)
    pallas_call x1, Pallas kernels, per_device(): pl.pallas_call(functools.partial(kernel, n, 1.0 / (owned * n)), out_shape...  88.2 us

profile of v1, /device:TPU:31, one launch (start us, length us, event | category | flops | bytes accessed | tf_op | source)
XLA Modules:
  0.0 96.0 jit_solution(12088195641464544185)
XLA Ops:
  0.0 0.6 copy-done.2
  0.7 0.1 dynamic_slice.21
  0.8 0.1 dynamic_slice.23
  0.8 0.1 dynamic-slice_compare_fusion
  0.9 0.1 ge.15
  1.0 0.1 mul.43
  1.1 0.1 mul.40
  1.2 0.1 lt.93
  1.3 0.1 lt.86
  1.3 0.4 convert_reduce_fusion
  1.8 0.1 copy.11
  1.8 0.6 select_reduce_fusion
  2.4 0.7 dynamic-slice_reduce_fusion.2.pick
  3.2 0.8 dynamic-slice_reduce_fusion
  3.9 0.1 copy.12
  4.0 0.1 copy.13
  4.1 0.1 lt.95
  4.2 0.1 lt.96
  4.3 0.1 lt.88
  4.3 0.1 lt.89
  4.4 0.6 broadcast_in_dim.2.mask_in
  5.1 0.9 fusion.2.w_in
  5.9 88.2 %shard_map.73 = f32[320,384]{1,0:T(8,128)} custom-call(s32[10]{0:T(128)} %dynamic-slice_reduce_fusion.2.pick, s32[10]{0:T(128)} %get-tuple-element.11.high, s32[10]{0:T(128)} %get-tuple-element.10.wide, bf16[10,64,640]{2,1,0:T(8,128)(2,1)} %bitcast.10, bf16[10,64,320]{2,1,0:T(8,128)(2,1)} %bitcast.11, bf16[8,80,384]{2,1,0:T(8,128)(2,1)} %fusion.2.w_in, ...), custom_call_target="tpu_custom_call" | custom-call | tf_op jit(solution)/shard_map/pallas_call | solution.py:396
  94.2 1.8 %slice_bitcast_fusion = f32[360,320]{0,1:T(8,128)} fusion(f32[320,384]{1,0:T(8,128)} %shard_map.73), kind=kLoop, calls=%fused_computation.4 | loop fusion | bytes 921600 | tf_op jit(solution)/shard_map/transpose | solution.py:414
  (14 shorter events, 0.0 us)
Async XLA Ops:
  0.0 0.7 copy-start.2
  0.0 0.8 copy-start.3
  0.0 0.8 copy-start.4
  0.0 5.1 %copy-start.1 = (bf16[360,320]{0,1:T(8,128)(2,1)S(1)}, bf16[360,320]{0,1:T(8,128)(2,1)}, u32[]{:S(2)}) copy-start(bf16[360,320]{0,1:T(8,128)(2,1)} %param.12) | copy-start | bytes 691204
  0.0 5.1 %copy-start = (bf16[360,320]{0,1:T(8,128)(2,1)S(1)}, bf16[360,320]{0,1:T(8,128)(2,1)}, u32[]{:S(2)}) copy-start(bf16[360,320]{0,1:T(8,128)(2,1)} %param.13) | copy-start | bytes 691204

commit v2 on v1

--- a/solution.py
+++ b/solution.py
@@ -149,12 +149,27 @@
             x / (1.0 + jnp.exp(-x)) * inside[k]
         ).astype(BF16)
 
-    def send_hidden(k, _):
-        target = base + lax.rem(pos + k, BLOCK)
-        remote(hid.at[pos], hid.at[pos], h_send, h_recv, target).start()
-        return 0
-
-    lax.fori_loop(1, BLOCK, send_hidden, 0)
+    side = chip + 1 - 2 * lax.rem(chip, 2)
+    ahead = lax.rem(chip + 2, CHIPS)
+    across = lax.rem(side + 2, CHIPS)
+    chips = (chip, side, ahead, across)
+
+    def pass_on(which, position, piece, target):
+        part = hid.at[position] if piece is None else hid.at[position, pl.ds(piece * quarter, quarter)]
+        copy = remote(part, part, h_send.at[which], h_recv.at[which], target)
+        copy.start()
+        return copy
+
+    quarter = half // 2
+    passed = [
+        pass_on(1, pos, None, base + 2 * side + core),
+        pass_on(2, pos, None, base + 2 * ahead + core),
+        pass_on(0, pos, None, partner),
+    ]
+
+    def arrived(which, piece):
+        part = hid.at[pos] if piece is None else hid.at[pos, pl.ds(piece * quarter, quarter)]
+        remote(part, part, h_send.at[which], h_recv.at[which], partner).wait_recv()
 
     tgt_copy.wait_recv()
     chosen = []
@@ -175,6 +190,13 @@
         return 0
 
     lax.fori_loop(1, CHIPS, send_targets, 0)
+
+    arrived(1, None)
+    passed.append(pass_on(3, 2 * side + core, 0, base + 2 * ahead + core))
+    passed.append(pass_on(5, 2 * side + core, None, partner))
+    arrived(2, None)
+    passed.append(pass_on(4, 2 * ahead + core, 1, base + 2 * side + core))
+    passed.append(pass_on(6, 2 * ahead + core, None, partner))
 
     remote(w_buf, w_buf, w_send, w_recv, partner).wait_recv()
     w_flat[...] = jnp.zeros_like(w_flat)
@@ -206,11 +228,7 @@
         )
         return a * 8 + b, valid.astype(F32)
 
-    remote(
-        hid.at[pl.ds(0, BLOCK - 1)], hid.at[pl.ds(0, BLOCK - 1)], h_send, h_recv, partner
-    ).wait_recv()
-
-    def forward(q, _):
+    def forward(q, place):
         features = hid[pl.ds(2 * q, 2)].reshape(width, channels)
         z[...] = lax.dot_general(
             wall[...], features, (((1,), (1,)), ((), ())), preferred_element_type=F32
@@ -222,16 +240,10 @@
                 total = total + valid * pltpu.roll(
                     z[tap * both : (tap + 1) * both], -offset % width, 1
                 )
-        u_buf[q] = total[:cols]
-        t_tan[q] = total[cols:]
-        return 0
-
-    lax.fori_loop(0, CHIPS, forward, 0)
-    remote(
-        t_buf.at[pl.ds(0, CHIPS - 1)], t_buf.at[pl.ds(0, CHIPS - 1)], t_send, t_recv, partner
-    ).wait_recv()
-
-    wide_rows = CHIPS * cols
+        u_buf[place * cols : (place + 1) * cols] = total[:cols]
+        t_tan[place * cols : (place + 1) * cols] = total[cols:]
+
+    wide_rows = 2 * cols
     to_sample = between(
         iota((width, LANES), 0), iota((width, LANES), 1), CELLS
     ).astype(F32).astype(BF16)
@@ -242,65 +254,99 @@
     to_norm = between(row, col, PER_GROUP).astype(F32).astype(BF16)
     row, col = iota((LANES, wide_rows), 1), iota((LANES, wide_rows), 0)
     of_norm = between(row, col, PER_GROUP).astype(F32).astype(BF16)
-    mask = jnp.concatenate(
-        [jnp.broadcast_to(mask_in[q, 0:1], (cols, width)) for q in range(CHIPS)], axis=0
-    )
-    per_sample = jnp.dot(mask.astype(BF16), to_sample, preferred_element_type=F32)
-    inverse = 1.0 / (jnp.maximum(per_sample, 1.0) * PER_GROUP)
-
-    def small(value):
-        return onehot_times(to_norm, onehot_times(of_norm, times_onehot(value, to_sample))) * inverse
-
-    def spread(value):
-        return times_onehot(value, from_sample)
-
-    u = u_buf[...].reshape(wide_rows, width)
-    t = t_tan[...].reshape(wide_rows, width)
-    c = u - spread(small(u * mask))
-    r = spread(lax.rsqrt(small(c * c * mask) + EPSILON))
-    x = c * r
-    wanted = jnp.concatenate([t_buf[q].astype(F32)[:cols] for q in range(CHIPS)], axis=0)
-    a = spread(small(x * t * mask))
-    x_dot = r * (t - spread(small(t * mask)) - x * a)
-    sigma = 1.0 / (1.0 + jnp.exp(-x))
-    missing = x * sigma - wanted
-    first = sigma * (1.0 + x * (1.0 - sigma))
-    second = sigma * (1.0 - sigma) * (2.0 + x * (1.0 - 2.0 * sigma))
-    weight = factor * mask
-    g = weight * missing * first
-    g_dot = weight * (first * first + missing * second) * x_dot
-    b = spread(small(g * x))
-    h = g - spread(small(g)) - x * b
-    h_dot = g_dot - spread(small(g_dot)) - x_dot * b - x * spread(small(g_dot * x + g * x_dot))
-    result = mask * (r * h_dot - r * r * a * h)
-    curv[...] = result.reshape(CHIPS, cols, width)
-
-    acc[...] = jnp.zeros_like(acc)
-
-    def backward(q, _):
-        values = curv[q]
+
+    def second_order(near, far):
+        mask = jnp.concatenate(
+            [jnp.broadcast_to(mask_in[q, 0:1], (cols, width)) for q in (near, far)], axis=0
+        )
+        per_sample = jnp.dot(mask.astype(BF16), to_sample, preferred_element_type=F32)
+        inverse = 1.0 / (jnp.maximum(per_sample, 1.0) * PER_GROUP)
+
+        def small(*values):
+            sums = times_onehot(jnp.concatenate(values, axis=0), to_sample)
+            sums = jnp.concatenate(
+                [sums[k * wide_rows : (k + 1) * wide_rows] for k in range(len(values))], axis=1
+            )
+            sums = onehot_times(to_norm, onehot_times(of_norm, sums))
+            return [
+                sums[:, k * LANES : (k + 1) * LANES] * inverse for k in range(len(values))
+            ]
+
+        def spread(*values):
+            back = times_onehot(jnp.concatenate(values, axis=0), from_sample)
+            return [back[k * wide_rows : (k + 1) * wide_rows] for k in range(len(values))]
+
+        u = u_buf[...]
+        t = t_tan[...]
+        u_mean, t_mean = spread(*small(u * mask, t * mask))
+        c = u - u_mean
+        (square,) = small(c * c * mask)
+        (r,) = spread(lax.rsqrt(square + EPSILON))
+        x = c * r
+        wanted = jnp.concatenate([t_buf[q].astype(F32)[:cols] for q in (near, far)], axis=0)
+        sigma = 1.0 / (1.0 + jnp.exp(-x))
+        missing = x * sigma - wanted
+        first = sigma * (1.0 + x * (1.0 - sigma))
+        second = sigma * (1.0 - sigma) * (2.0 + x * (1.0 - 2.0 * sigma))
+        weight = factor * mask
+        g = weight * missing * first
+        a, g_mean, b = spread(*small(x * t * mask, g, g * x))
+        x_dot = r * (t - t_mean - x * a)
+        g_dot = weight * (first * first + missing * second) * x_dot
+        h = g - g_mean - x * b
+        g_dot_mean, b_dot = spread(*small(g_dot, g_dot * x + g * x_dot))
+        h_dot = g_dot - g_dot_mean - x_dot * b - x * b_dot
+        curv[...] = mask * (r * h_dot - r * r * a * h)
+
+    def backward(q, place, adds):
+        values = curv[place * cols : (place + 1) * cols]
         shifted = []
         for tap in range(9):
             offset, valid = tap_of(tap)
             term = values * valid
             shifted.append(term if offset == 0 else pltpu.roll(term, offset % width, 1))
         features = hid[pl.ds(2 * q, 2)].reshape(width, channels)
-        acc[...] += jnp.dot(
+        product = jnp.dot(
             jnp.concatenate(shifted, axis=0).astype(BF16), features, preferred_element_type=F32
         )
-        return 0
-
-    lax.fori_loop(0, CHIPS, backward, 0)
+        acc[...] = acc[...] + product if adds else product
+
+    arrived(0, None)
+    forward(chip, 0)
+    arrived(5, None)
+    forward(side, 1)
+    remote(
+        t_buf.at[pl.ds(0, CHIPS - 1)], t_buf.at[pl.ds(0, CHIPS - 1)], t_send, t_recv, partner
+    ).wait_recv()
+    second_order(chip, side)
+    arrived(3, 0)
+    passed.append(pass_on(7, 2 * across + core, 0, partner))
+    arrived(4, 1)
+    passed.append(pass_on(8, 2 * across + core, 1, partner))
+    backward(chip, 0, False)
+    backward(side, 1, True)
+    arrived(6, None)
+    forward(ahead, 0)
+    arrived(7, 0)
+    arrived(8, 1)
+    forward(across, 1)
+    second_order(ahead, across)
+    backward(ahead, 0, True)
+    backward(across, 1, True)
     flat = w_flat
     for tap in range(9):
         flat[:cols, tap * channels : (tap + 1) * channels] = acc[tap * cols : (tap + 1) * cols]
+    tiles = rows // LANES
     r_rows = r_out.shape[1]
     for d in range(n):
         start, size = window_of(d * share, share, kernel_rows)
-        piece = flat[: r_rows, start : start + size]
+        piece = flat[:cols, start : start + size]
         if d * share > start:
             piece = pltpu.roll(piece, (start - d * share) % size, 1)
-        r_out[d] = piece[:, :rows].astype(BF16)
+        stacked = [piece[:, k * LANES : (k + 1) * LANES] for k in range(tiles)]
+        if r_rows > tiles * cols:
+            stacked.append(jnp.zeros((r_rows - tiles * cols, LANES), F32))
+        r_out[d] = jnp.concatenate(stacked, axis=0).astype(BF16)
 
     def send_sums(k, _):
         target = lax.rem(me + k, n)
@@ -315,16 +361,19 @@
         total = r_buf[b].astype(F32)
         for other in range(b + BLOCK, n, BLOCK):
             total = total + r_buf[other].astype(F32)
-        out[b * cols : (b + 1) * cols] = total[:cols]
+        for k in range(tiles):
+            out[b * cols : (b + 1) * cols, k * LANES : (k + 1) * LANES] = total[
+                k * cols : (k + 1) * cols
+            ]
 
     lat_copy.wait_send()
     tgt_copy.wait_send()
     others = pl.ds(0, n - 1)
     remote(w_buf.at[others], w_buf.at[others], w_send, w_recv, partner).wait_send()
-    peers = pl.ds(0, BLOCK - 1)
-    remote(hid.at[peers], hid.at[peers], h_send, h_recv, partner).wait_send()
-    chips = pl.ds(0, CHIPS - 1)
-    remote(t_buf.at[chips], t_buf.at[chips], t_send, t_recv, partner).wait_send()
+    for copy in passed:
+        copy.wait_send()
+    three = pl.ds(0, CHIPS - 1)
+    remote(t_buf.at[three], t_buf.at[three], t_send, t_recv, partner).wait_send()
     remote(r_buf.at[others], r_buf.at[others], r_send, r_recv, partner).wait_send()
 
 
@@ -386,13 +435,13 @@
         pltpu.VMEM((BLOCK, padded, width), BF16),
         pltpu.VMEM((CHIPS, padded, width), BF16),
         pltpu.VMEM((9 * 2 * cols, width), F32),
-        pltpu.VMEM((CHIPS, cols, width), F32),
-        pltpu.VMEM((CHIPS, cols, width), F32),
-        pltpu.VMEM((CHIPS, cols, width), F32),
+        pltpu.VMEM((2 * cols, width), F32),
+        pltpu.VMEM((2 * cols, width), F32),
+        pltpu.VMEM((2 * cols, width), F32),
         pltpu.VMEM((9 * cols, channels), F32),
-        pltpu.VMEM((n, padded, rows), BF16),
-        pltpu.VMEM((n, padded, rows), BF16),
-    ] + [sem] * 12
+        pltpu.VMEM((n, up(cols * rows // LANES, 16), LANES), BF16),
+        pltpu.VMEM((n, up(cols * rows // LANES, 16), LANES), BF16),
+    ] + [sem] * 6 + [sem((9,))] * 2 + [sem] * 4
     turned = pl.pallas_call(
         functools.partial(kernel, n, 1.0 / (owned * n)),
         out_shape=jax.ShapeDtypeStruct((out_channels, rows), F32),

time: 96.4 us -> 71.6 us (0.74)
  Pallas kernels: 88.2 us -> 63.6 us
    pallas_call x1, Pallas kernels: 88.2 us -> 63.6 us  [per_device(): pl.pallas_call(functools.partial(kernel, n, 1.0 / (owned * n)), out_shape...]
where the time goes in v2:
time: 71.6 us; the launch traced here: 71.4 us
  Pallas kernels  63.6 us (89%)
  local copies, waits for them, and re-layouts  5.75 us (8%)
  other arithmetic  1.96 us (3%)
    pallas_call x1, Pallas kernels, per_device(): pl.pallas_call(functools.partial(kernel, n, 1.0 / (owned * n)), out_shape...  63.6 us
    transpose x1, local copies, waits for them, and re-layouts, per_device(): return turned[:, :share].T  1.84 us
    dynamic_slice x2, local copies, waits for them, and re-layouts, mine(): return lax.dynamic_index_in_dim(values, chip, 0, keepdims=False)  1.5 us

profile of v2, /device:TPU:31, one launch (start us, length us, event | category | flops | bytes accessed | tf_op | source)
XLA Modules:
  0.0 71.4 jit_solution(4213561859658413378)
XLA Ops:
  0.0 0.6 copy-done.2
  0.7 0.1 dynamic_slice.21
  0.8 0.1 dynamic_slice.23
  0.8 0.1 dynamic-slice_compare_fusion
  0.9 0.1 ge.15
  1.0 0.1 mul.43
  1.1 0.1 mul.40
  1.2 0.1 lt.93
  1.3 0.1 lt.86
  1.3 0.4 convert_reduce_fusion
  1.8 0.1 copy.11
  1.8 0.6 select_reduce_fusion
  2.4 0.7 %dynamic-slice_reduce_fusion.2.pick = s32[10]{0:T(128)} fusion(s32[4,10]{0,1:T(8,128)S(1)} %get-tuple-element.7, s32[]{:T(128)S(6)} %select_n.43), kind=kLoop, calls=%fused_computation.15 | loop fusion | bytes 84 | tf_op jit(solution)/shard_map/jit(dynamic_index_in_dim)/dynamic_slice | solution.py:418
  3.2 0.8 %dynamic-slice_reduce_fusion = (s32[10]{0:T(128)}, s32[10]{0:T(128)}) fusion(s32[4,10]{0,1:T(8,128)S(1)} %get-tuple-element.5, s32[]{:T(128)S(6)} %select_n.43, s32[4,10]{0,1:T(8,128)S(1)} %get-tuple-element.6), kind=kLoop, calls=%fused_computation.13 | loop fusion | bytes 164 | tf_op jit(solution)/shard_map/jit(dynamic_index_in_dim)/dynamic_slice | solution.py:418
  3.9 0.1 copy.12
  4.0 0.1 copy.13
  4.1 0.1 lt.95
  4.2 0.1 lt.96
  4.3 0.1 lt.88
  4.3 0.1 lt.89
  4.4 0.6 broadcast_in_dim.2.mask_in
  5.1 0.9 %fusion.2.w_in = bf16[8,80,384]{2,1,0:T(8,128)(2,1)} fusion(bf16[8,40,360]{2,1,0:T(8,128)(2,1)S(1)} %bitcast.12, bf16[8,40,360]{2,1,0:T(8,128)(2,1)S(1)} %bitcast.13), kind=kLoop, calls=%fused_computation.3 | loop fusion | flops 1720320 | bytes 952320 | tf_op jit(solution)/shard_map/concatenate | solution.py:420
  5.9 63.6 %shard_map.73 = f32[320,384]{1,0:T(8,128)} custom-call(s32[10]{0:T(128)} %dynamic-slice_reduce_fusion.2.pick, s32[10]{0:T(128)} %get-tuple-element.11.high, s32[10]{0:T(128)} %get-tuple-element.10.wide, bf16[10,64,640]{2,1,0:T(8,128)(2,1)} %bitcast.10, bf16[10,64,320]{2,1,0:T(8,128)(2,1)} %bitcast.11, bf16[8,80,384]{2,1,0:T(8,128)(2,1)} %fusion.2.w_in, ...), custom_call_target="tpu_custom_call" | custom-call | tf_op jit(solution)/shard_map/pallas_call | solution.py:445
  69.6 1.8 %slice_bitcast_fusion = f32[360,320]{0,1:T(8,128)} fusion(f32[320,384]{1,0:T(8,128)} %shard_map.73), kind=kLoop, calls=%fused_computation.4 | loop fusion | bytes 921600 | tf_op jit(solution)/shard_map/transpose | solution.py:463
  (14 shorter events, 0.0 us)
Async XLA Ops:
  0.0 0.7 copy-start.2
  0.0 0.8 %copy-start.3 = (s32[160]{0:T(256)S(1)}, s32[160]{0:T(256)}, u32[]{:S(2)}) copy-start(s32[160]{0:T(256)} %param.10) | copy-start | bytes 1924
  0.0 0.8 %copy-start.4 = (s32[160]{0:T(256)S(1)}, s32[160]{0:T(256)}, u32[]{:S(2)}) copy-start(s32[160]{0:T(256)} %param.11) | copy-start | bytes 1924
  0.0 5.1 %copy-start.1 = (bf16[360,320]{0,1:T(8,128)(2,1)S(1)}, bf16[360,320]{0,1:T(8,128)(2,1)}, u32[]{:S(2)}) copy-start(bf16[360,320]{0,1:T(8,128)(2,1)} %param.12) | copy-start | bytes 691204
  0.0 5.1 %copy-start = (bf16[360,320]{0,1:T(8,128)(2,1)S(1)}, bf16[360,320]{0,1:T(8,128)(2,1)}, u32[]{:S(2)}) copy-start(bf16[360,320]{0,1:T(8,128)(2,1)} %param.13) | copy-start | bytes 691204

commit v3 on v2

--- a/solution.py
+++ b/solution.py
@@ -59,7 +59,7 @@
 
 
 def kernel(
-    n, factor, pick, high, wide, lat_in, tgt_in, w_in, mask_in, out,
+    n, factor, table, lat_in, tgt_in, w_in, mask_in, out,
     lat, tgt, w_buf, w_flat, wall, hid, t_out, t_buf, z, u_buf, t_tan, curv, acc, r_out, r_buf,
     lat_send, lat_recv, tgt_send, tgt_recv, w_send, w_recv, h_send, h_recv, t_send, t_recv,
     r_send, r_recv,
@@ -126,8 +126,9 @@
     cell_row, cell_col = cell >> 3, cell & 7
     frames, inside, counts = [], [], []
     for k in range(owned):
-        which = pick[core * owned + k]
-        tall, broad = high[core * owned + k], wide[core * owned + k]
+        which, tall, broad = (
+            table[(CHIPS * field + chip) * pair + core * owned + k] for field in range(3)
+        )
         frames.append(lat[which // slots, lax.rem(which, slots)].astype(F32))
         inside.append(((cell_row < tall) & (cell_col < broad)).astype(F32))
         counts.append(jnp.full((1, LANES), tall * broad * PER_GROUP, jnp.int32).astype(F32))
@@ -155,12 +156,13 @@
     chips = (chip, side, ahead, across)
 
     def pass_on(which, position, piece, target):
-        part = hid.at[position] if piece is None else hid.at[position, pl.ds(piece * quarter, quarter)]
+        part = hid.at[position] if piece is None else hid.at[position, pieces[piece]]
         copy = remote(part, part, h_send.at[which], h_recv.at[which], target)
         copy.start()
         return copy
 
-    quarter = half // 2
+    small_part = half // 4
+    pieces = (pl.ds(0, small_part), pl.ds(small_part, half - small_part))
     passed = [
         pass_on(1, pos, None, base + 2 * side + core),
         pass_on(2, pos, None, base + 2 * ahead + core),
@@ -168,13 +170,13 @@
     ]
 
     def arrived(which, piece):
-        part = hid.at[pos] if piece is None else hid.at[pos, pl.ds(piece * quarter, quarter)]
+        part = hid.at[pos] if piece is None else hid.at[pos, pieces[piece]]
         remote(part, part, h_send.at[which], h_recv.at[which], partner).wait_recv()
 
     tgt_copy.wait_recv()
     chosen = []
     for k in range(pair):
-        which = pick[k]
+        which = table[chip * pair + k]
         chosen.append(tgt[which // slots, lax.rem(which, slots)].astype(F32))
     turned = jnp.concatenate(chosen, axis=0).T
     t_rows = t_out.shape[1]
@@ -243,21 +245,21 @@
         u_buf[place * cols : (place + 1) * cols] = total[:cols]
         t_tan[place * cols : (place + 1) * cols] = total[cols:]
 
-    wide_rows = 2 * cols
     to_sample = between(
         iota((width, LANES), 0), iota((width, LANES), 1), CELLS
     ).astype(F32).astype(BF16)
     from_sample = between(
         iota((LANES, width), 1), iota((LANES, width), 0), CELLS
     ).astype(F32).astype(BF16)
-    row, col = iota((wide_rows, LANES), 0), iota((wide_rows, LANES), 1)
-    to_norm = between(row, col, PER_GROUP).astype(F32).astype(BF16)
-    row, col = iota((LANES, wide_rows), 1), iota((LANES, wide_rows), 0)
-    of_norm = between(row, col, PER_GROUP).astype(F32).astype(BF16)
-
-    def second_order(near, far):
+
+    def second_order(*those):
+        wide_rows = len(those) * cols
+        row, col = iota((wide_rows, LANES), 0), iota((wide_rows, LANES), 1)
+        to_norm = between(row, col, PER_GROUP).astype(F32).astype(BF16)
+        row, col = iota((LANES, wide_rows), 1), iota((LANES, wide_rows), 0)
+        of_norm = between(row, col, PER_GROUP).astype(F32).astype(BF16)
         mask = jnp.concatenate(
-            [jnp.broadcast_to(mask_in[q, 0:1], (cols, width)) for q in (near, far)], axis=0
+            [jnp.broadcast_to(mask_in[q, 0:1], (cols, width)) for q in those], axis=0
         )
         per_sample = jnp.dot(mask.astype(BF16), to_sample, preferred_element_type=F32)
         inverse = 1.0 / (jnp.maximum(per_sample, 1.0) * PER_GROUP)
@@ -276,14 +278,14 @@
             back = times_onehot(jnp.concatenate(values, axis=0), from_sample)
             return [back[k * wide_rows : (k + 1) * wide_rows] for k in range(len(values))]
 
-        u = u_buf[...]
-        t = t_tan[...]
+        u = u_buf[:wide_rows]
+        t = t_tan[:wide_rows]
         u_mean, t_mean = spread(*small(u * mask, t * mask))
         c = u - u_mean
         (square,) = small(c * c * mask)
         (r,) = spread(lax.rsqrt(square + EPSILON))
         x = c * r
-        wanted = jnp.concatenate([t_buf[q].astype(F32)[:cols] for q in (near, far)], axis=0)
+        wanted = jnp.concatenate([t_buf[q].astype(F32)[:cols] for q in those], axis=0)
         sigma = 1.0 / (1.0 + jnp.exp(-x))
         missing = x * sigma - wanted
         first = sigma * (1.0 + x * (1.0 - sigma))
@@ -296,7 +298,7 @@
         h = g - g_mean - x * b
         g_dot_mean, b_dot = spread(*small(g_dot, g_dot * x + g * x_dot))
         h_dot = g_dot - g_dot_mean - x_dot * b - x * b_dot
-        curv[...] = mask * (r * h_dot - r * r * a * h)
+        curv[:wide_rows] = mask * (r * h_dot - r * r * a * h)
 
     def backward(q, place, adds):
         values = curv[place * cols : (place + 1) * cols]
@@ -318,21 +320,21 @@
     remote(
         t_buf.at[pl.ds(0, CHIPS - 1)], t_buf.at[pl.ds(0, CHIPS - 1)], t_send, t_recv, partner
     ).wait_recv()
-    second_order(chip, side)
+    arrived(6, None)
+    forward(ahead, 2)
+    second_order(chip, side, ahead)
     arrived(3, 0)
     passed.append(pass_on(7, 2 * across + core, 0, partner))
     arrived(4, 1)
     passed.append(pass_on(8, 2 * across + core, 1, partner))
     backward(chip, 0, False)
     backward(side, 1, True)
-    arrived(6, None)
-    forward(ahead, 0)
+    backward(ahead, 2, True)
     arrived(7, 0)
     arrived(8, 1)
-    forward(across, 1)
-    second_order(ahead, across)
-    backward(ahead, 0, True)
-    backward(across, 1, True)
+    forward(across, 0)
+    second_order(across)
+    backward(across, 0, True)
     flat = w_flat
     for tap in range(9):
         flat[:cols, tap * channels : (tap + 1) * channels] = acc[tap * cols : (tap + 1) * cols]
@@ -403,19 +405,17 @@
     taken = (
         (rank[:, None, :] == jnp.arange(pair, dtype=jnp.int32)[None, :, None]) & live[:, None, :]
     ).astype(jnp.int32)
-    slot = jnp.sum(taken * index[None, None, :], axis=2)
-    tall = jnp.sum(taken * of_block(heights)[:, None, :], axis=2)
-    broad = jnp.sum(taken * of_block(widths)[:, None, :], axis=2)
+    fields = jnp.stack(
+        [jnp.broadcast_to(index, (CHIPS, 2 * slots)), of_block(heights), of_block(widths)]
+    )
+    table = jnp.sum(taken[None] * fields[:, :, None, :], axis=3)
+    tall, broad = table[1], table[2]
     place = jnp.arange(cells, dtype=jnp.int32)
     mask = (
         (place[None, None, :] // frame_cols < tall[:, :, None])
         & (place[None, None, :] % frame_cols < broad[:, :, None])
     ).astype(F32)
     mask = jnp.broadcast_to(mask.reshape(CHIPS, 1, width), (CHIPS, 8, width))
-    chip = (me - base) // 2
-
-    def mine(values):
-        return lax.dynamic_index_in_dim(values, chip, 0, keepdims=False)
 
     both = jnp.concatenate(
         [weight.T.reshape(BLOCK, cols, share), probe.T.reshape(BLOCK, cols, share)], axis=1
@@ -435,9 +435,9 @@
         pltpu.VMEM((BLOCK, padded, width), BF16),
         pltpu.VMEM((CHIPS, padded, width), BF16),
         pltpu.VMEM((9 * 2 * cols, width), F32),
-        pltpu.VMEM((2 * cols, width), F32),
-        pltpu.VMEM((2 * cols, width), F32),
-        pltpu.VMEM((2 * cols, width), F32),
+        pltpu.VMEM((3 * cols, width), F32),
+        pltpu.VMEM((3 * cols, width), F32),
+        pltpu.VMEM((3 * cols, width), F32),
         pltpu.VMEM((9 * cols, channels), F32),
         pltpu.VMEM((n, up(cols * rows // LANES, 16), LANES), BF16),
         pltpu.VMEM((n, up(cols * rows // LANES, 16), LANES), BF16),
@@ -445,16 +445,14 @@
     turned = pl.pallas_call(
         functools.partial(kernel, n, 1.0 / (owned * n)),
         out_shape=jax.ShapeDtypeStruct((out_channels, rows), F32),
-        in_specs=[smem] * 3 + [vmem] * 4,
+        in_specs=[smem] + [vmem] * 4,
         out_specs=vmem,
         scratch_shapes=scratch,
         compiler_params=pltpu.CompilerParams(
             collective_id=0, has_side_effects=True, vmem_limit_bytes=56 * 2**20
         ),
     )(
-        mine(slot),
-        mine(tall),
-        mine(broad),
+        table.reshape(3 * CHIPS * pair),
         latents.reshape(slots, cells, channels),
         targets.reshape(slots, cells, out_channels),
         both,

time: 71.6 us -> 72.5 us (1.013)
    dynamic_slice x2 -> x0, local copies, waits for them, and re-layouts: 1.5 us -> none  [mine(): return lax.dynamic_index_in_dim(values, chip, 0, keepdims=False)]
    unnamed x10, local copies, waits for them, and re-layouts: 0.65 us -> 1.89 us
where the time goes in v3:
time: 72.5 us; the launch traced here: 72.3 us
  Pallas kernels  64 us (88%)
  local copies, waits for them, and re-layouts  6.2 us (9%)
  other arithmetic  1.98 us (3%)
    pallas_call x1, Pallas kernels, per_device(): pl.pallas_call(functools.partial(kernel, n, 1.0 / (owned * n)), out_shape...  64 us
    unnamed x10, local copies, waits for them, and re-layouts  1.89 us
    transpose x1, local copies, waits for them, and re-layouts, per_device(): return turned[:, :share].T  1.84 us

profile of v3, /device:TPU:31, one launch (start us, length us, event | category | flops | bytes accessed | tf_op | source)
XLA Modules:
  0.0 72.3 jit_solution(15586459984192878947)
XLA Ops:
  0.0 0.7 copy-done.2
  0.7 0.1 dynamic_slice.10
  0.8 0.6 copy-done.3
  1.4 0.1 dynamic_slice.11
  1.4 0.6 copy-done.4
  2.0 0.1 dynamic-slice_compare_fusion
  2.1 0.1 ge.15
  2.2 0.1 stack_reshape.7
  2.3 0.1 stack_reshape.6
  2.6 0.4 convert_reduce_fusion
  3.0 0.1 copy.8
  3.1 0.6 multiply_reduce_fusion
  3.7 0.1 copy.9
  3.8 0.6 reshape.127.table
  4.4 0.1 copy.10
  4.5 0.1 copy.11
  4.6 0.1 lt.94
  4.6 0.1 lt.95
  4.7 0.1 lt.86
  4.8 0.1 lt.87
  4.9 0.6 broadcast_in_dim.2.mask_in
  5.5 0.9 %fusion.2.w_in = bf16[8,80,384]{2,1,0:T(8,128)(2,1)} fusion(bf16[8,40,360]{2,1,0:T(8,128)(2,1)S(1)} %bitcast.14, bf16[8,40,360]{2,1,0:T(8,128)(2,1)S(1)} %bitcast.15), kind=kLoop, calls=%fused_computation.3 | loop fusion | flops 1720320 | bytes 952320 | tf_op jit(solution)/shard_map/concatenate | solution.py:420
  6.4 64.0 %shard_map.73 = f32[320,384]{1,0:T(8,128)} custom-call(s32[120]{0:T(128)} %reshape.127.table, bf16[10,64,640]{2,1,0:T(8,128)(2,1)} %bitcast.12, bf16[10,64,320]{2,1,0:T(8,128)(2,1)} %bitcast.13, bf16[8,80,384]{2,1,0:T(8,128)(2,1)} %fusion.2.w_in, f32[4,8,640]{2,1,0:T(8,128)} %broadcast_in_dim.2.mask_in), custom_call_target="tpu_custom_call" | custom-call | tf_op jit(solution)/shard_map/pallas_call | solution.py:445
  70.4 1.8 %slice_bitcast_fusion = f32[360,320]{0,1:T(8,128)} fusion(f32[320,384]{1,0:T(8,128)} %shard_map.73), kind=kLoop, calls=%fused_computation.4 | loop fusion | bytes 921600 | tf_op jit(solution)/shard_map/transpose | solution.py:461
  (19 shorter events, 0.2 us)
Async XLA Ops:
  0.0 0.7 copy-start.2
  0.7 0.7 copy-start.3
  1.4 0.7 copy-start.4
  2.5 3.0 %copy-start.1 = (bf16[360,320]{0,1:T(8,128)(2,1)S(1)}, bf16[360,320]{0,1:T(8,128)(2,1)}, u32[]{:S(2)}) copy-start(bf16[360,320]{0,1:T(8,128)(2,1)} %param.12) | copy-start | bytes 691204
  2.6 3.0 %copy-start = (bf16[360,320]{0,1:T(8,128)(2,1)S(1)}, bf16[360,320]{0,1:T(8,128)(2,1)}, u32[]{:S(2)}) copy-start(bf16[360,320]{0,1:T(8,128)(2,1)} %param.13) | copy-start | bytes 691204
